TPU v7x, 256 devices: a whole 4x4x8 slice. The times are simulated.
256 devices in a mesh: dp: 16 (over y, x), graph: 16 (over z, core).
Axes of the slice: x: 4, y: 4, z: 8, core: 2. Of those that a mesh axis runs over, the one named last changes fastest.
Arguments:
- edge_in: bfloat16 [262144, 512], P(('dp', 'graph')), may hold values from -6 to 6
- cotangent: bfloat16 [262144, 512], P(('dp', 'graph')), may hold values from -6 to 6
- weight_first: bfloat16 [512, 512], replicated, may hold values from -0.25 to 0.25
- weight_second: bfloat16 [512, 512], replicated, may hold values from -0.25 to 0.25
- weight_down: bfloat16 [64, 512], replicated, may hold values from -0.25 to 0.25
- weight_up: bfloat16 [64, 512], replicated, may hold values from -0.75 to 0.75
- coeffs: bfloat16 [6144, 128, 128], P(('dp', 'graph')), may hold values from -0.29882812 to 0.29882812
- tile_source: int32 [6144], P(('dp', 'graph')), may hold values from 0 to 127
- tile_target: int32 [6144], P(('dp', 'graph')), may hold values from 0 to 7
- tile_count: int32 [256], P(('dp', 'graph')), may hold values from 8 to 24, as said below
Outputs:
- edge_grad: bfloat16 [262144, 512], P(('dp', 'graph'))
- grad_first: float32 [512, 512], replicated
- grad_second: float32 [512, 512], replicated
- grad_down: float32 [64, 512], replicated
- grad_up: float32 [64, 512], replicated
Inputs may be any that keep to these rules, and one draw needn't show every extreme that they name: `tile_count`: slots of a device at or beyond its count are padding: their sources, targets and coefficients are ignored. In every graph batch some device has exactly 24 live slots.
All inputs are finite; a program needn't handle non-finite values.
Results may differ from a plain program's by a relative error of at most 0.019.
Values may be sent and summed in bfloat16 or wider, within the bound.
A program may use at most 128 MiB of HBM per device.

v0:
```python
import jax
import jax.numpy as jnp
from jax import lax
from jax.sharding import PartitionSpec as P


def silu_grad(values):
    sigma = jax.nn.sigmoid(values)
    return sigma * (1.0 + values * (1.0 - sigma))


def on_device(
    edge_in,
    cotangent,
    weight_first,
    weight_second,
    weight_down,
    weight_up,
    coeffs,
    tile_source,
    tile_target,
    tile_count,
):
    edge_rows = edge_in.shape[0]
    tiles_dev = edge_rows // 128
    channels = weight_down.shape[0]
    groups = lax.axis_size("graph")
    tiles_all = groups * tiles_dev
    slot_total = tile_source.shape[0]
    contract_last = (((1,), (1,)), ((), ()))
    contract_first = (((0,), (0,)), ((), ()))
    pre_first = jnp.dot(edge_in, weight_first, preferred_element_type=jnp.float32)
    hidden_one = jax.nn.silu(pre_first).astype(jnp.bfloat16)
    pre_second = jnp.dot(hidden_one, weight_second, preferred_element_type=jnp.float32)
    states = (edge_in.astype(jnp.float32) + jax.nn.silu(pre_second)).astype(jnp.bfloat16)
    states_all = lax.all_gather(states, "graph", axis=0, tiled=True)
    pre_all = lax.dot_general(
        weight_down, states_all, contract_last, preferred_element_type=jnp.float32
    )
    projected_all = jax.nn.silu(pre_all).astype(jnp.bfloat16)
    pre_down = lax.dynamic_slice_in_dim(pre_all, lax.axis_index("graph") * edge_rows, edge_rows, 1)
    usable = (jnp.arange(slot_total) < tile_count[0]).astype(jnp.bfloat16)
    source_rows = jnp.take(projected_all.reshape(channels, tiles_all, 128), tile_source, axis=1)
    source_rows = source_rows * usable[None, :, None]
    contrib = jnp.einsum("cks,kts->ckt", source_rows, coeffs, preferred_element_type=jnp.float32)
    target_hot = (tile_target[:, None] == jnp.arange(tiles_dev)[None, :]).astype(jnp.float32)
    aggregate = jnp.einsum("ckt,kj->cjt", contrib, target_hot, precision=lax.Precision.HIGHEST)
    aggregate = aggregate.reshape(channels, edge_rows).astype(jnp.bfloat16)
    pre_up = lax.dot_general(
        aggregate, weight_up, contract_first, preferred_element_type=jnp.float32
    )
    up_cot = (cotangent.astype(jnp.float32) * silu_grad(pre_up)).astype(jnp.bfloat16)
    grad_up = jnp.dot(aggregate, up_cot, preferred_element_type=jnp.float32)
    agg_cot = lax.dot_general(
        weight_up, up_cot, contract_last, preferred_element_type=jnp.float32
    ).astype(jnp.bfloat16)
    target_rows = jnp.take(agg_cot.reshape(channels, tiles_dev, 128), tile_target, axis=1)
    target_rows = target_rows * usable[None, :, None]
    back = jnp.einsum("ckt,kts->cks", target_rows, coeffs, preferred_element_type=jnp.float32)
    source_hot = (tile_source[:, None] == jnp.arange(tiles_all)[None, :]).astype(jnp.float32)
    spread = jnp.einsum("cks,kj->cjs", back, source_hot, precision=lax.Precision.HIGHEST)
    spread = spread.reshape(channels, tiles_all * 128)
    source_cot = lax.psum_scatter(
        spread.astype(jnp.bfloat16), "graph", scatter_dimension=1, tiled=True
    ).astype(jnp.float32)
    down_cot = (source_cot * silu_grad(pre_down)).astype(jnp.bfloat16)
    grad_down = jnp.dot(down_cot, states, preferred_element_type=jnp.float32)
    state_cot = cotangent.astype(jnp.float32) + lax.dot_general(
        down_cot, weight_down, contract_first, preferred_element_type=jnp.float32
    )
    second_cot = (state_cot * silu_grad(pre_second)).astype(jnp.bfloat16)
    grad_second = lax.dot_general(
        hidden_one, second_cot, contract_first, preferred_element_type=jnp.float32
    )
    hidden_cot = lax.dot_general(
        second_cot, weight_second, contract_last, preferred_element_type=jnp.float32
    )
    first_cot = (hidden_cot * silu_grad(pre_first)).astype(jnp.bfloat16)
    grad_first = lax.dot_general(
        edge_in, first_cot, contract_first, preferred_element_type=jnp.float32
    )
    edge_grad = (
        state_cot
        + lax.dot_general(
            first_cot, weight_first, contract_last, preferred_element_type=jnp.float32
        )
    ).astype(jnp.bfloat16)
    summed = lax.psum((grad_first, grad_second, grad_down, grad_up), ("dp", "graph"))
    return (edge_grad, summed[0], summed[1], summed[2], summed[3])


def solution(mesh):
    return jax.shard_map(
        on_device,
        mesh=mesh,
        in_specs=(
            P(("dp", "graph"), None),
            P(("dp", "graph"), None),
            P(),
            P(),
            P(),
            P(),
            P(("dp", "graph"), None, None),
            P(("dp", "graph")),
            P(("dp", "graph")),
            P(("dp", "graph")),
        ),
        out_specs=(P(("dp", "graph"), None), P(), P(), P(), P()),
        check_vma=False,
    )
```

profile of v0, /device:TPU:1, one launch (start us, length us, event | category | flops | bytes accessed | tf_op | source)
XLA Modules:
  0.0 475.6 jit_solution(15330009047997201573)
XLA Ops:
  7.2 3.8 multiply_convert_fusion.2
  11.1 2.6 add_convert_fusion.1
  14.5 99.0 %all-gather.2.cloned.1.call-done = bf16[16384,512]{1,0:T(8,128)(2,1)} async-done(((bf16[1024,512]{1,0:T(8,128)(2,1)}), bf16[16384,512]{1,0:T(8,128)(2,1)}) %all-gather.2.cloned.1.call-update) | async-done | bytes 16777232 | tf_op jit(solution)/shard_map/all_gather | solution.py:36
  113.5 10.9 %fusion.48 = f32[16384,64]{0,1:T(8,128)S(1)} fusion(bf16[16384,512]{1,0:T(8,128)(2,1)} %all-gather.2.cloned.1.call-done, bf16[64,512]{1,0:T(8,128)(2,1)S(1)} %copy-done.8), kind=kOutput, calls=%fused_computation.75 | convolution fusion | flops 1073741824 | bytes 21037056 | tf_op jit(solution)/shard_map/dot_general | solution.py:37
  124.4 2.0 copy-done.1
  126.3 1.1 copy_bitcast_fusion.1
  128.1 0.7 fusion.13
  128.8 0.8 convolution_convert_fusion.2
  129.6 1.0 fusion.4
  132.1 2.0 convolution_convert_fusion
  134.1 2.8 copy.44
  137.1 1.0 fusion.32
  138.1 53.4 %reduce-scatter.2.cloned.1.call-done = bf16[64,1024]{1,0:T(8,128)(2,1)} async-done(((bf16[64,16384]{1,0:T(8,128)(2,1)}), bf16[64,1024]{1,0:T(8,128)(2,1)}) %reduce-scatter.2.cloned.1.call-update) | async-done | bytes 131088 | tf_op jit(solution)/shard_map/reduce_scatter | solution.py:63
  191.5 3.1 multiply_convert_fusion.1
  194.6 1.7 fusion.49
  196.4 1.2 multiply_convert_fusion
  197.6 1.7 convolution_bitcast_fusion
  199.4 2.0 fusion.45
  201.4 2.9 add_convert_fusion
  204.3 259.8 %all-reduce.3.cloned.1.call-done = (f32[512,512]{0,1:T(8,128)}, f32[512,512]{1,0:T(8,128)}, f32[64,512]{1,0:T(8,128)}, f32[64,512]{1,0:T(8,128)}) async-done(((f32[512,512]{0,1:T(8,128)}, f32[512,512]{1,0:T(8,128)}, f32[64,512]{1,0:T(8,128)}, f32[64,512]{1,0:T(8,128)}), (f32[512,512]{0,1:T(8,128)}, f32[512,512]{1,0:T(8,128)}, f32[64,512]{1,0:T(8,128)}, f32[64,512]{1,0:T(8,128)})) %all-reduce.3.cloned.1.call-update) | async-done | bytes 2359312 | tf_op jit(solution)/shard_map/psum | solution.py:88
  464.1 2.6 copy.18
  466.8 1.0 copy.51
  467.7 0.7 copy.52
  468.4 0.7 copy.53
  (58 shorter events, 2.7 us)
Async XLA Ops:
  7.2 120.9 %copy-start = (bf16[24,128,128]{2,1,0:T(8,128)(2,1)S(1)}, bf16[24,128,128]{2,1,0:T(8,128)(2,1)}, u32[]{:S(2)}) copy-start(bf16[24,128,128]{2,1,0:T(8,128)(2,1)} %param.16) | copy-start | bytes 2359300
  7.2 3.8 copy-start.13
  7.2 3.8 copy-start.15
  7.2 106.3 %all-gather.2.cloned.1.call-start = ((), (), s32[]{:S(2)}) async-start(), calls=%async_computation.1 | async-start | bytes 17825792 | tf_op jit(solution)/shard_map/all_gather | solution.py:36
  11.0 2.6 copy-start.18
  11.0 3.3 copy-start.10
  11.0 3.4 copy-start.11
  11.1 102.4 %copy-start.8 = (bf16[64,512]{1,0:T(8,128)(2,1)S(1)}, bf16[64,512]{1,0:T(8,128)(2,1)}, u32[]{:S(2)}) copy-start(bf16[64,512]{1,0:T(8,128)(2,1)} %param.14) | copy-start | bytes 196612
  13.7 177.8 %reduce-scatter.2.cloned.1.call-start = ((), (), s32[]{:S(2)}) async-start(), calls=%async_computation.2 | async-start | bytes 2228224 | tf_op jit(solution)/shard_map/reduce_scatter | solution.py:63
  124.4 2.0 copy-start.1
  127.4 2.2 copy-start.9
  128.1 1.5 copy-start.12
  136.9 327.2 %all-reduce.3.cloned.1.call-start = ((), (), s32[]{:S(2)}) async-start(), calls=%async_computation.3 | async-start | bytes 4718592 | tf_op jit(solution)/shard_map/psum | solution.py:88
  191.5 3.1 copy-start.19
  194.6 1.8 copy-start.16
  194.6 1.8 copy-start.20
  196.4 1.2 copy-start.14
  197.6 1.7 copy-start.4
  197.6 1.7 copy-start.2
  197.6 1.7 copy-start.17
  199.4 2.0 copy-start.5
  464.1 2.6 copy-start.3
  464.1 3.6 copy-start.7
  464.1 4.3 copy-start.6
Sparse Core Ops, SparseCore 0:
  13.8 99.6 all-gather.1
  137.0 54.4 reduce-scatter.1
  201.5 262.6 all-reduce.2
where the time goes:
time: 477 us; the launch traced here: 476 us
  waiting for transfers between devices  412 us (86%)
  matrix products  36.1 us (8%)
  between operations  14.7 us (3%)
  local copies, waits for them, and re-layouts  11.1 us (2%)
    psum x1, waiting for transfers between devices, on_device(): lax.psum((grad_first, grad_second, grad_down, grad_up), ('dp', 'graph'))  260 us
    all_gather x1, waiting for transfers between devices, on_device(): states_all = lax.all_gather(states, 'graph', axis=0, tiled=True)  99 us
    reduce_scatter x1, waiting for transfers between devices, on_device(): lax.psum_scatter(spread.astype(jnp.bfloat16), 'graph', scatter_dimension=...  53.4 us
    dot_general x1, matrix products, on_device(): lax.dot_general(weight_down, states_all, contract_last, preferred_element...  10.9 us
    unnamed x47, local copies, waits for them, and re-layouts  9.85 us
  transfers between devices with their start and end apart: 3, of which 3 were waited for; matrix products, arithmetic and copies ran while one was open for 1% of the time, Pallas kernels for 0%

commit v1 on v0

v1 whole, which is shorter than its diff:
```python
import functools

import jax
import jax.numpy as jnp
from jax import lax
from jax.experimental import pallas as pl
from jax.experimental.pallas import tpu as pltpu
from jax.sharding import PartitionSpec as P

F32 = jnp.float32
BF16 = jnp.bfloat16
MESH = pl.DeviceIdType.MESH
LAST = (((1,), (1,)), ((), ()))
FIRST = (((0,), (0,)), ((), ()))

NX, NY, NZ = 4, 4, 8
HALF = NZ // 2
D, TW = 512, 64
ROWS, TILE, TILES, SLOTS = 1024, 128, 8, 24
CH = 2
NCH = TILES // CH
RB = CH * TILE
EXTRA = TILE
WB = D + EXTRA


def sigmoid(v):
    return 0.5 * jnp.tanh(0.5 * v) + 0.5


def silu_grad(v):
    s = sigmoid(v)
    return s * (1.0 + v * (1.0 - s))


def dot(a, b):
    return jnp.dot(a, b, preferred_element_type=F32)


def dotg(a, b, dims):
    return lax.dot_general(a, b, dims, preferred_element_type=F32)


def rows_at(start, size, step):
    return pl.ds(pl.multiple_of(start, step), size)


class AllReduce:
    def __init__(self, place, loc, refs, sems):
        self.p = place
        self.loc = loc
        self.snd1, self.rcv1, self.acc, self.snd2, self.rcv2, self.acc3, self.snd3, self.rcv3, self.z4, self.fin = refs
        self.ssem, self.rsem = sems
        self.open = []

    def copy(self, src, dst, idx, dev):
        return pltpu.make_async_remote_copy(
            src_ref=src, dst_ref=dst, send_sem=self.ssem.at[idx], recv_sem=self.rsem.at[idx],
            device_id=dev, device_id_type=MESH,
        )

    def start(self, src, dst, idx, dev):
        c = self.copy(src, dst, idx, dev)
        c.start()
        self.open.append(c)

    def arrived(self, dst, idx):
        self.copy(dst, dst, idx, self.p.sib).wait_recv()

    def p1(self):
        p = self.p
        h = D // 2
        self.snd1[...] = self.loc[rows_at((1 - p.c) * h, h, h), :].astype(BF16)
        self.start(self.snd1, self.rcv1, 0, p.sib)

    def p2(self):
        p = self.p
        h, q = D // 2, D // 2 // NX
        self.arrived(self.rcv1, 0)
        acc = self.loc[rows_at(p.c * h, h, h), :] + self.rcv1[...].astype(F32)
        self.acc[...] = acc
        self.snd2[...] = acc.astype(BF16)
        for d in range(1, NX):
            xt = lax.rem(p.x + d, NX)
            self.start(self.snd2.at[rows_at(xt * q, q, q)], self.rcv2.at[p.x], d, (p.y * NX + xt, p.g))

    def p3(self):
        p = self.p
        q, r = D // 2 // NX, D // 2 // NX // NY
        acc = self.acc[rows_at(p.x * q, q, q), :]
        for d in range(1, NX):
            xs = lax.rem(p.x + NX - d, NX)
            self.arrived(self.rcv2.at[xs], d)
            acc = acc + self.rcv2[xs].astype(F32)
        self.acc3[...] = acc
        self.snd3[...] = acc.astype(BF16)
        for d in range(1, NY):
            yt = lax.rem(p.y + d, NY)
            self.start(self.snd3.at[rows_at(yt * r, r, r)], self.rcv3.at[p.y], 3 + d, (yt * NX + p.x, p.g))

    def p4(self):
        p = self.p
        r = D // 2 // NX // NY
        acc = self.acc3[rows_at(p.y * r, r, r), :]
        for d in range(1, NY):
            ys = lax.rem(p.y + NY - d, NY)
            self.arrived(self.rcv3.at[ys], 3 + d)
            acc = acc + self.rcv3[ys].astype(F32)
        self.z4[p.z] = acc.astype(BF16)
        for d in (4, 3, 5, 2, 6, 1, 7):
            zt = lax.rem(p.z + d, NZ)
            self.start(self.z4.at[p.z], self.z4.at[p.z], 6 + d, (p.dp, zt * 2 + p.c))

    def mine(self, start, size):
        return self.fin.at[rows_at(start, size, size)]

    def p5(self):
        p = self.p
        r = D // 2 // NX // NY
        for d in range(1, NZ):
            zs = lax.rem(p.z + NZ - d, NZ)
            self.arrived(self.z4.at[zs], 6 + d)
        acc = self.z4[0].astype(F32)
        for i in range(1, NZ):
            acc = acc + self.z4[i].astype(F32)
        base = (p.c * NX + p.x) * NY
        self.fin[rows_at((base + p.y) * r, r, r), :] = acc.astype(BF16)
        for d in range(1, NY):
            yt = lax.rem(p.y + d, NY)
            part = self.mine((base + p.y) * r, r)
            self.start(part, part, 13 + d, (yt * NX + p.x, p.g))

    def p6(self):
        p = self.p
        q, r = D // 2 // NX, D // 2 // NX // NY
        base = (p.c * NX + p.x) * NY
        for d in range(1, NY):
            ys = lax.rem(p.y + NY - d, NY)
            self.arrived(self.mine((base + ys) * r, r), 13 + d)
        part = self.mine((p.c * NX + p.x) * q, q)
        for d in range(1, NX):
            xt = lax.rem(p.x + d, NX)
            self.start(part, part, 16 + d, (p.y * NX + xt, p.g))

    def p7(self):
        p = self.p
        h, q = D // 2, D // 2 // NX
        for d in range(1, NX):
            xs = lax.rem(p.x + NX - d, NX)
            self.arrived(self.mine((p.c * NX + xs) * q, q), 16 + d)
        part = self.mine(p.c * h, h)
        self.start(part, part, 20, p.sib)

    def p8(self):
        h = D // 2
        self.arrived(self.mine((1 - self.p.c) * h, h), 20)

    def close(self):
        for c in self.open:
            c.wait_send()


class Place:
    def __init__(self):
        self.dp = lax.axis_index("dp")
        self.g = lax.axis_index("graph")
        self.y, self.x = lax.div(self.dp, NX), lax.rem(self.dp, NX)
        self.z, self.c = lax.div(self.g, 2), lax.rem(self.g, 2)
        self.sib = (self.dp, self.z * 2 + 1 - self.c)

    def zdev(self, off):
        return (self.dp, self.zat(off) * 2 + self.c)

    def zat(self, off):
        return lax.rem(self.z + off + NZ, NZ)

    def partners(self):
        out = [self.sib]
        out += [self.zdev(d) for d in range(1, NZ)]
        out += [(self.y * NX + lax.rem(self.x + d, NX), self.g) for d in range(1, NX)]
        out += [(lax.rem(self.y + d, NY) * NX + self.x, self.g) for d in range(1, NY)]
        return out


def kernel(
    ts, tt, tc, x_hbm, g_hbm, w1_hbm, w2_hbm, wd_hbm, wu_hbm, co_hbm,
    eg_hbm, a_hbm, b_hbm,
    x, g, w1, w2, wd, wu, co, in_sem,
    d1, d2, h1t, xt, states, pd, proj, ag_s, ag_r, as_s, as_r,
    sl, tl, prev_s, prev_t, last_t, idx,
    comb, agg, upcot, aggcot,
    sib_snd, sib_rcv, rs_snd, rs_rcv, rb_s, rb_r, rr_s, rr_r,
    downcot, sc, second, first, ga, gb, eg, eg_sem, out_sem,
    *ar,
):
    p = Place()
    loads = [
        pltpu.make_async_copy(s, t, in_sem.at[i])
        for i, (s, t) in enumerate(
            ((x_hbm, x), (w1_hbm, w1), (w2_hbm, w2), (wd_hbm, wd), (co_hbm, co), (wu_hbm, wu), (g_hbm, g))
        )
    ]
    for c in loads:
        c.start()
    barrier = pltpu.get_barrier_semaphore()
    partners = p.partners()
    for dev in partners:
        pl.semaphore_signal(barrier, inc=1, device_id=dev, device_id_type=MESH)
    pl.semaphore_wait(barrier, len(partners))
    opened = []

    def block(zi, core, ch, n=CH):
        return proj.at[pl.ds((zi * 2 + core) * TILES + ch * CH, n)]

    def ring(side, step, ch):
        b = block(p.zat(-step if side == 0 else step), p.c, ch)
        return pltpu.make_async_remote_copy(
            src_ref=b, dst_ref=b, send_sem=ag_s.at[side, step, ch], recv_sem=ag_r.at[side, step, ch],
            device_id=p.zdev(1 if side == 0 else -1), device_id_type=MESH,
        )

    def ring_arrival(side, step, ch):
        b = block(p.zat(-1 - step if side == 0 else 1 + step), p.c, ch)
        pltpu.make_async_remote_copy(
            src_ref=b, dst_ref=b, send_sem=ag_s.at[side, step, ch], recv_sem=ag_r.at[side, step, ch],
            device_id=p.sib, device_id_type=MESH,
        ).wait_recv()

    def share(off, ch, core):
        b = block(p.zat(off), core, ch)
        k = off % NZ
        return pltpu.make_async_remote_copy(
            src_ref=b, dst_ref=b, send_sem=as_s.at[k, ch], recv_sem=as_r.at[k, ch],
            device_id=p.sib, device_id_type=MESH,
        )

    for i in range(4):
        loads[i].wait()

    @pl.loop(0, NCH)
    def _(i):
        rows = rows_at(i * RB, RB, RB)
        m = x[rows, :]
        v1 = dot(m, w1[...])
        h = (v1 * sigmoid(v1)).astype(BF16)
        d1[rows, :] = v1
        v2 = dot(h, w2[...])
        st = (m.astype(F32) + v2 * sigmoid(v2)).astype(BF16)
        d2[rows, :] = v2
        first[rows, :] = h
        states[rows, :] = st
        vd = dotg(wd[...], st, LAST)
        pr = (vd * sigmoid(vd)).astype(BF16)
        for j in range(CH):
            pd[i * CH + j] = vd[:, j * TILE:(j + 1) * TILE]
            proj[p.g * TILES + i * CH + j] = pr[:, j * TILE:(j + 1) * TILE]
        ring(0, 0, i).start()
        ring(1, 0, i).start()
        share(0, i, p.c).start()

    count = tc[0]
    for k in range(SLOTS):
        live = k < count
        sl[k] = jnp.where(live, ts[k], -1)
        tl[k] = jnp.where(live, tt[k], -1)
    for k in range(SLOTS):
        a = jnp.int32(SLOTS)
        b = jnp.int32(SLOTS)
        for e in range(k):
            a = jnp.where(sl[e] == ts[k], e, a)
            b = jnp.where(tl[e] == tt[k], e, b)
        prev_s[k] = a
        prev_t[k] = b
    for j in range(TILES):
        a = jnp.int32(SLOTS)
        for k in range(SLOTS):
            a = jnp.where(tl[k] == j, k, a)
        last_t[j] = a

    def tables(lo, hi):
        @pl.loop(lo, hi)
        def _(j):
            a = jnp.int32(SLOTS)
            for k in range(SLOTS):
                a = jnp.where(sl[k] == j, k, a)
            idx[j] = a

    def side_work(i):
        rows = rows_at(i * RB, RB, RB)
        d1[rows, :] = silu_grad(d1[rows, :])
        d2[rows, :] = silu_grad(d2[rows, :])
        h1t[:, rows] = first[rows, :].T
        xt[:, rows] = x[rows, :].T

    comb[SLOTS] = jnp.zeros((TW, TILE), F32)

    for s in range(HALF):
        for ch in range(NCH):
            for side in (0, 1):
                lower = ch < NCH // 2
                mine = (side == 0) == lower
                if s == HALF - 1 and not mine:
                    continue
                ring_arrival(side, s, ch)
                if s + 1 < HALF - 1 or (s + 1 == HALF - 1 and mine):
                    ring(side, s + 1, ch).start()
                share(-1 - s if side == 0 else 1 + s, ch, p.c).start()
        if s < HALF:
            side_work(s)
            tables(s * 32, s * 32 + 32)

    for off in range(NZ):
        for ch in range(NCH):
            share(off, ch, 1 - p.c).wait_recv()

    loads[4].wait()
    for k in range(SLOTS):
        part = dotg(proj[ts[k]], co[k], LAST)
        comb[k] = part + comb[prev_t[k]]
    for j in range(TILES):
        agg[:, j * TILE:(j + 1) * TILE] = comb[last_t[j]].astype(BF16)

    loads[5].wait()
    loads[6].wait()

    @pl.loop(0, NCH)
    def _(i):
        rows = rows_at(i * RB, RB, RB)
        pu = dotg(agg[:, rows], wu[...], FIRST)
        uc = (g[rows, :].astype(F32) * silu_grad(pu)).astype(BF16)
        upcot[rows, :] = uc
        ac = dotg(wu[...], uc, LAST).astype(BF16)
        for j in range(CH):
            aggcot[i * CH + j] = ac[:, j * TILE:(j + 1) * TILE]

    for k in range(SLOTS):
        part = dot(aggcot[tt[k]], co[k])
        comb[k] = part + comb[prev_s[k]]

    def sib_copy(off):
        k = off % NZ
        return pltpu.make_async_remote_copy(
            src_ref=sib_snd.at[k], dst_ref=sib_rcv.at[k], send_sem=rb_s.at[k], recv_sem=rb_r.at[k],
            device_id=p.sib, device_id_type=MESH,
        )

    order = (4, 3, -3, 2, -2, 1, -1, 0)
    for off in order:
        base = (p.zat(off) * 2 + 1 - p.c) * TILES
        k = off % NZ

        @pl.loop(0, TILES)
        def _(j):
            sib_snd[k, j] = comb[idx[base + j]].astype(BF16)

        sib_copy(off).start()

    def red(side, step, ch):
        return pltpu.make_async_remote_copy(
            src_ref=rs_snd.at[side, step, pl.ds(ch * CH, CH)], dst_ref=rs_rcv.at[side, step, pl.ds(ch * CH, CH)],
            send_sem=rr_s.at[side, step, ch], recv_sem=rr_r.at[side, step, ch],
            device_id=p.zdev(1 if side == 0 else -1), device_id_type=MESH,
        )

    for s in range(HALF):
        for side in (0, 1):
            off = HALF - s if side == 0 else s - HALF
            base = (p.zat(off) * 2 + p.c) * TILES
            if s > 0 or side == 0:
                sib_copy(off).wait_recv()
            for ch in range(NCH):
                mine = (side == 0) == (ch < NCH // 2)
                if s == 0 and not mine:
                    continue
                more = s > 1 or (s == 1 and mine)
                if more:
                    red(side, s - 1, ch).wait_recv()
                for j in range(ch * CH, ch * CH + CH):
                    v = comb[idx[base + j]] + sib_rcv[off % NZ, j].astype(F32)
                    if more:
                        v = v + rs_rcv[side, s - 1, j].astype(F32)
                    rs_snd[side, s, j] = v.astype(BF16)
                red(side, s, ch).start()
        if s == 0:
            gu = dot(agg[...], upcot[...])
            for b in range(D // TILE):
                gb[b * TILE:b * TILE + TW, D:] = gu[:, b * TILE:(b + 1) * TILE]

    sib_copy(0).wait_recv()
    base = p.g * TILES
    for ch in range(NCH):
        red(0, HALF - 1, ch).wait_recv()
        red(1, HALF - 1, ch).wait_recv()
        for j in range(ch * CH, ch * CH + CH):
            v = comb[idx[base + j]] + sib_rcv[0, j].astype(F32)
            v = v + rs_rcv[0, HALF - 1, j].astype(F32) + rs_rcv[1, HALF - 1, j].astype(F32)
            downcot[:, j * TILE:(j + 1) * TILE] = (v * silu_grad(pd[j])).astype(BF16)

    @pl.loop(0, NCH)
    def _(i):
        rows = rows_at(i * RB, RB, RB)
        v = g[rows, :].astype(F32) + dotg(downcot[:, rows], wd[...], FIRST)
        sc[rows, :] = v
        second[rows, :] = (v * d2[rows, :]).astype(BF16)

    @pl.loop(0, D // 256)
    def _(i):
        rows = rows_at(i * 256, 256, 256)
        gb[rows, :D] = dot(h1t[rows, :], second[...])

    gd = dot(downcot[...], states[...])
    for b in range(D // TILE):
        gb[b * TILE + TW:(b + 1) * TILE, D:] = gd[:, b * TILE:(b + 1) * TILE]

    n = len(ar) // 2
    ar_a = AllReduce(p, ga, ar[:n - 2], ar[n - 2:n])
    ar_b = AllReduce(p, gb, ar[n:2 * n - 2], ar[2 * n - 2:])
    ar_b.p1()

    @pl.loop(0, NCH)
    def _(i):
        rows = rows_at(i * RB, RB, RB)
        v = dotg(second[rows, :], w2[...], LAST)
        first[rows, :] = (v * d1[rows, :]).astype(BF16)

    ar_b.p2()

    @pl.loop(0, D // 256)
    def _(i):
        rows = rows_at(i * 256, 256, 256)
        ga[rows, :] = dot(xt[rows, :], first[...])

    ar_a.p1()
    ar_b.p3()

    def eg_copy(i):
        rows = rows_at(i * RB, RB, RB)
        return pltpu.make_async_copy(eg.at[rows, :], eg_hbm.at[rows, :], eg_sem.at[i])

    def edges(lo, hi):
        @pl.loop(lo, hi)
        def _(i):
            rows = rows_at(i * RB, RB, RB)
            v = sc[rows, :] + dotg(first[rows, :], w1[...], LAST)
            eg[rows, :] = v.astype(BF16)
            eg_copy(i).start()

    ar_a.p2()
    ar_b.p4()
    edges(0, NCH // 2)
    ar_a.p3()
    ar_b.p5()
    edges(NCH // 2, NCH)
    ar_a.p4()
    ar_b.p6()
    ar_a.p5()
    ar_b.p7()
    ar_a.p6()
    ar_b.p8()
    ob = pltpu.make_async_copy(ar_b.fin, b_hbm, out_sem.at[1])
    ob.start()
    ar_a.p7()
    ar_a.p8()
    oa = pltpu.make_async_copy(ar_a.fin, a_hbm, out_sem.at[0])
    oa.start()

    for ch in range(NCH):
        for side in (0, 1):
            for s in range(HALF):
                mine = (side == 0) == (ch < NCH // 2)
                if s < HALF - 1 or mine:
                    ring(side, s, ch).wait_send()
                if s > 0 or mine:
                    red(side, s, ch).wait_send()
        for off in range(NZ):
            share(off, ch, p.c).wait_send()
        eg_copy(ch).wait()
    for off in range(NZ):
        sib_copy(off).wait_send()
    ar_a.close()
    ar_b.close()
    ob.wait()
    oa.wait()


def ar_scratch(w):
    h, q, r = D // 2, D // 2 // NX, D // 2 // NX // NY
    return [
        pltpu.VMEM((h, w), BF16), pltpu.VMEM((h, w), BF16), pltpu.VMEM((h, w), F32), pltpu.VMEM((h, w), BF16),
        pltpu.VMEM((NX, q, w), BF16), pltpu.VMEM((q, w), F32), pltpu.VMEM((q, w), BF16),
        pltpu.VMEM((NY, r, w), BF16), pltpu.VMEM((NZ, r, w), BF16), pltpu.VMEM((D, w), BF16),
        pltpu.SemaphoreType.DMA((21,)), pltpu.SemaphoreType.DMA((21,)),
    ]


def on_device(
    edge_in, cotangent, weight_first, weight_second, weight_down, weight_up,
    coeffs, tile_source, tile_target, tile_count,
):
    V, S = pltpu.VMEM, pltpu.SMEM
    dma = pltpu.SemaphoreType.DMA
    scratch = [
        V((ROWS, D), BF16), V((ROWS, D), BF16), V((D, D), BF16), V((D, D), BF16),
        V((TW, D), BF16), V((TW, D), BF16), V((SLOTS, TILE, TILE), BF16), dma((7,)),
        V((ROWS, D), F32), V((ROWS, D), F32), V((D, ROWS), BF16), V((D, ROWS), BF16),
        V((ROWS, D), BF16), V((TILES, TW, TILE), F32), V((2 * NZ * TILES, TW, TILE), BF16),
        dma((2, HALF, NCH)), dma((2, HALF, NCH)), dma((NZ, NCH)), dma((NZ, NCH)),
        S((SLOTS,), jnp.int32), S((SLOTS,), jnp.int32), S((SLOTS,), jnp.int32), S((SLOTS,), jnp.int32),
        S((TILES,), jnp.int32), S((2 * NZ * TILES,), jnp.int32),
        V((SLOTS + 1, TW, TILE), F32), V((TW, ROWS), BF16), V((ROWS, D), BF16), V((TILES, TW, TILE), BF16),
        V((NZ, TILES, TW, TILE), BF16), V((NZ, TILES, TW, TILE), BF16),
        V((2, HALF, TILES, TW, TILE), BF16), V((2, HALF, TILES, TW, TILE), BF16),
        dma((NZ,)), dma((NZ,)), dma((2, HALF, NCH)), dma((2, HALF, NCH)),
        V((TW, ROWS), BF16), V((ROWS, D), F32), V((ROWS, D), BF16), V((ROWS, D), BF16),
        V((D, D), F32), V((D, WB), F32), V((ROWS, D), BF16), dma((NCH,)), dma((2,)),
    ] + ar_scratch(D) + ar_scratch(WB)
    hbm = pl.BlockSpec(memory_space=pl.ANY)
    smem = pl.BlockSpec(memory_space=pltpu.SMEM)
    edge_grad, a, b = pl.pallas_call(
        kernel,
        out_shape=(
            jax.ShapeDtypeStruct((ROWS, D), BF16),
            jax.ShapeDtypeStruct((D, D), BF16),
            jax.ShapeDtypeStruct((D, WB), BF16),
        ),
        in_specs=[smem] * 3 + [hbm] * 7,
        out_specs=(hbm,) * 3,
        scratch_shapes=scratch,
        compiler_params=pltpu.CompilerParams(
            collective_id=0, has_side_effects=True, vmem_limit_bytes=56 * 1024 * 1024
        ),
        cost_estimate=pl.CostEstimate(flops=7_400_000_000, bytes_accessed=8_000_000, transcendentals=2_000_000),
    )(
        tile_source, tile_target, tile_count, edge_in, cotangent, weight_first, weight_second,
        weight_down, weight_up, coeffs,
    )
    extra = b[:, D:].reshape(D // TILE, 2, TW, TILE).transpose(1, 2, 0, 3).reshape(2, TW, D).astype(F32)
    return (edge_grad, a.astype(F32), b[:, :D].astype(F32), extra[1], extra[0])


def solution(mesh):
    return jax.shard_map(
        on_device,
        mesh=mesh,
        in_specs=(
            P(("dp", "graph"), None), P(("dp", "graph"), None), P(), P(), P(), P(),
            P(("dp", "graph"), None, None), P(("dp", "graph")), P(("dp", "graph")), P(("dp", "graph")),
        ),
        out_specs=(P(("dp", "graph"), None), P(), P(), P(), P()),
        check_vma=False,
    )
```

time: 477 us -> 95.7 us (0.20)
  waiting for transfers between devices: 412 us -> 0 us
  Pallas kernels: 0 us -> 88.5 us
  matrix products: 36.1 us -> 0 us
  between operations: 14.7 us -> 1.34 us
  local copies, waits for them, and re-layouts: 11.1 us -> 3.48 us
    psum x1 -> x0, waiting for transfers between devices: 260 us -> none  [on_device(): lax.psum((grad_first, grad_second, grad_down, grad_up), ('dp', 'graph'))]
    all_gather x1 -> x0, waiting for transfers between devices: 99 us -> none  [on_device(): states_all = lax.all_gather(states, 'graph', axis=0, tiled=True)]
    pallas_call x0 -> x1, Pallas kernels: none -> 88.5 us  [on_device(): pl.pallas_call(kernel, out_shape=(jax.ShapeDtypeStruct((ROWS, D), BF16),...]
    reduce_scatter x1 -> x0, waiting for transfers between devices: 53.4 us -> none  [on_device(): lax.psum_scatter(spread.astype(jnp.bfloat16), 'graph', scatter_dimension=...]
    dot_general x16 -> x0, matrix products: 36.1 us -> none  [the longest x1 10.9 us: on_device(): lax.dot_general(weight_down, states_all, contract_last, preferred_element...]
    unnamed x47 -> x7, local copies, waits for them, and re-layouts: 9.85 us -> 1.65 us
  transfers between devices with their start and end apart: 3 -> 0, of which waited for: 3 -> 0; matrix products, arithmetic and copies ran while one was open for 1% -> 0% of each run, Pallas kernels for 0% -> 0%
where the time goes in v1:
time: 95.7 us; the launch traced here: 95.5 us
  Pallas kernels  88.5 us (92%)
  local copies, waits for them, and re-layouts  3.48 us (4%)
  other arithmetic  2.22 us (2%)
  between operations  1.34 us (1%)
    pallas_call x1, Pallas kernels, on_device(): pl.pallas_call(kernel, out_shape=(jax.ShapeDtypeStruct((ROWS, D), BF16),...  88.5 us
    convert_element_type x2, other arithmetic, on_device(): return (edge_grad, a.astype(F32), b[:, :D].astype(F32), extra[1], extra[0])  2.2 us

profile of v1, /device:TPU:1, one launch (start us, length us, event | category | flops | bytes accessed | tf_op | source)
XLA Modules:
  0.0 95.5 jit_solution(3443116980838937781)
XLA Ops:
  1.3 88.5 %shard_map.137 = (bf16[1024,512]{1,0:T(8,128)(2,1)}, bf16[512,512]{1,0:T(8,128)(2,1)}, bf16[512,640]{1,0:T(8,128)(2,1)}) custom-call(s32[24]{0:T(128)} %ts.1, s32[24]{0:T(128)} %tt.1, s32[1]{0:T(128)S(6)} %copy.22.tc, bf16[1024,512]{1,0:T(8,128)(2,1)} %x_hbm.1, bf16[1024,512]{1,0:T(8,128)(2,1)} %g_hbm.1, bf16[512,512]{1,0:T(8,128)(2,1)} %w1_hbm.1, ...), custom_call_target="tpu_custom_call" | custom-call | flops 7400000000 | bytes 8000000 | tf_op jit(solution)/shard_map/pallas_call | solution.py:519
  89.8 0.9 slice.15
  90.7 0.0 copy-start.1
  90.8 0.1 copy.16
  90.8 0.1 copy.15
  90.9 0.7 copy_bitcast_fusion
  91.7 0.2 copy-done.1
  91.8 0.0 copy-start.2
  91.8 1.1 %slice_convert_fusion = f32[512,512]{1,0:T(8,128)} fusion(bf16[512,640]{1,0:T(8,128)(2,1)S(1)} %copy-done.1), kind=kLoop, calls=%fused_computation | loop fusion | flops 262144 | bytes 1572864 | tf_op jit(solution)/shard_map/convert_element_type | solution.py:538
  92.9 0.0 copy-done.2
  92.9 0.0 copy-start
  92.9 1.1 %convert_element_type.16 = f32[512,512]{1,0:T(8,128)} convert(bf16[512,512]{1,0:T(8,128)(2,1)S(1)} %copy-done.2) | non-fusion elementwise | flops 262144 | bytes 1572864 | tf_op jit(solution)/shard_map/convert_element_type | solution.py:538
  94.0 0.5 copy-done
  94.5 1.0 %copy.23 = bf16[1024,512]{1,0:T(8,128)(2,1)} copy(bf16[1024,512]{1,0:T(8,128)(2,1)S(1)} %copy-done) | data formatting | bytes 2097152
  (2 shorter events, 0.0 us)
Async XLA Ops:
  90.7 1.1 %copy-start.1 = (bf16[512,640]{1,0:T(8,128)(2,1)S(1)}, bf16[512,640]{1,0:T(8,128)(2,1)}, u32[]{:S(2)}) copy-start(bf16[512,640]{1,0:T(8,128)(2,1)} %get-tuple-element.10) | copy-start | bytes 1966084
  91.8 1.1 %copy-start.2 = (bf16[512,512]{1,0:T(8,128)(2,1)S(1)}, bf16[512,512]{1,0:T(8,128)(2,1)}, u32[]{:S(2)}) copy-start(bf16[512,512]{1,0:T(8,128)(2,1)} %get-tuple-element.9) | copy-start | bytes 1572868
  92.9 1.6 %copy-start = (bf16[1024,512]{1,0:T(8,128)(2,1)S(1)}, bf16[1024,512]{1,0:T(8,128)(2,1)}, u32[]{:S(2)}) copy-start(bf16[1024,512]{1,0:T(8,128)(2,1)} %get-tuple-element.20) | copy-start | bytes 3145732

commit v2 on v1

v2 whole, which is shorter than its diff:
```python
import jax
import jax.numpy as jnp
from jax import lax
from jax.experimental import pallas as pl
from jax.experimental.pallas import tpu as pltpu
from jax.sharding import PartitionSpec as P

F32 = jnp.float32
BF16 = jnp.bfloat16
MESH = pl.DeviceIdType.MESH
LAST = (((1,), (1,)), ((), ()))
FIRST = (((0,), (0,)), ((), ()))

NX, NY, NZ = 4, 4, 8
HALF = NZ // 2
D, TW = 512, 64
ROWS, TILE, TILES, SLOTS = 1024, 128, 8, 24
CH = 2
NCH = TILES // CH
RB = CH * TILE
EXTRA = TILE
WB = D + EXTRA
N_DP = NX * NY
PIECE = D // 2 // N_DP
FAR_FIRST = sorted(range(1, N_DP), key=lambda e: (-(min(e // NX, NY - e // NX) + min(e % NX, NX - e % NX)), e))


def sigmoid(v):
    return 0.5 * jnp.tanh(0.5 * v) + 0.5


def silu_grad(v):
    s = sigmoid(v)
    return s * (1.0 + v * (1.0 - s))


def dot(a, b):
    return jnp.dot(a, b, preferred_element_type=F32)


def dotg(a, b, dims):
    return lax.dot_general(a, b, dims, preferred_element_type=F32)


def rows_at(start, size, step):
    return pl.ds(pl.multiple_of(start, step), size)


class AllReduce:
    def __init__(self, place, refs, sems):
        self.p = place
        self.snd1, self.rcv1, self.acc, self.snd2, self.rcv2, self.zs, self.fin = refs
        self.ssem, self.rsem = sems
        self.open = []

    def copy(self, src, dst, idx, dev):
        return pltpu.make_async_remote_copy(
            src_ref=src, dst_ref=dst, send_sem=self.ssem.at[idx], recv_sem=self.rsem.at[idx],
            device_id=dev, device_id_type=MESH,
        )

    def start(self, src, dst, idx, dev):
        c = self.copy(src, dst, idx, dev)
        c.start()
        self.open.append(c)

    def arrived(self, dst, idx):
        self.copy(dst, dst, idx, self.p.sib).wait_recv()

    def to_sibling(self):
        self.start(self.snd1, self.rcv1, 0, self.p.sib)

    def to_plane(self):
        p = self.p
        self.arrived(self.rcv1, 0)
        acc = self.acc[...] + self.rcv1[...].astype(F32)
        self.acc[...] = acc
        self.snd2[...] = acc.astype(BF16)
        for e in FAR_FIRST:
            to = p.dpat(e)
            self.start(self.snd2.at[rows_at(to * PIECE, PIECE, PIECE)], self.rcv2.at[p.dp], e, (to, p.g))

    def to_column(self):
        p = self.p
        acc = self.acc[rows_at(p.dp * PIECE, PIECE, PIECE), :]
        for e in FAR_FIRST[::-1]:
            frm = p.dpat(-e)
            self.arrived(self.rcv2.at[frm], e)
            acc = acc + self.rcv2[frm].astype(F32)
        self.zs[p.z] = acc.astype(BF16)
        for d in (4, 3, 5, 2, 6, 1, 7):
            self.start(self.zs.at[p.z], self.zs.at[p.z], 15 + d, p.zdev(d))

    def part(self, core, first, n):
        return self.fin.at[rows_at((core * N_DP + first) * PIECE, n * PIECE, n * PIECE)]

    def plane_back(self):
        p = self.p
        for d in (1, 7, 2, 6, 3, 5, 4):
            self.arrived(self.zs.at[p.zat(-d)], 15 + d)
        acc = self.zs[0].astype(F32)
        for i in range(1, NZ):
            acc = acc + self.zs[i].astype(F32)
        self.fin[rows_at((p.c * N_DP + p.dp) * PIECE, PIECE, PIECE), :] = acc.astype(BF16)
        mine = self.part(p.c, p.dp, 1)
        for e in FAR_FIRST:
            self.start(mine, mine, 22 + e, (p.dpat(e), p.g))

    def sibling_back(self):
        p = self.p
        for dy in (0, 1, 3, 2):
            for dx in (1, 3, 2, 0):
                e = dy * NX + dx
                if e:
                    self.arrived(self.part(p.c, p.dpat(-e), 1), 22 + e)
            ys = lax.rem(p.y + NY - dy, NY)
            group = self.part(p.c, ys * NX, NX)
            self.start(group, group, 38 + dy, p.sib)

    def end(self):
        p = self.p
        for dy in (0, 1, 3, 2):
            ys = lax.rem(p.y + NY - dy, NY)
            self.arrived(self.part(1 - p.c, ys * NX, NX), 38 + dy)

    def close(self):
        for c in self.open:
            c.wait_send()


class Place:
    def __init__(self):
        self.dp = lax.axis_index("dp")
        self.g = lax.axis_index("graph")
        self.y, self.x = lax.div(self.dp, NX), lax.rem(self.dp, NX)
        self.z, self.c = lax.div(self.g, 2), lax.rem(self.g, 2)
        self.sib = (self.dp, self.z * 2 + 1 - self.c)

    def zdev(self, off):
        return (self.dp, self.zat(off) * 2 + self.c)

    def zat(self, off):
        return lax.rem(self.z + off + NZ, NZ)

    def dpat(self, e):
        sign = 1 if e >= 0 else -1
        dy, dx = abs(e) // NX * sign, abs(e) % NX * sign
        return lax.rem(self.y + dy + NY, NY) * NX + lax.rem(self.x + dx + NX, NX)

    def partners(self):
        out = [self.sib]
        out += [self.zdev(d) for d in range(1, NZ)]
        out += [(self.dpat(e), self.g) for e in range(1, N_DP)]
        return out


def kernel(
    ts_hbm, tt_hbm, tc_hbm, x_hbm, g_hbm, w1_hbm, w2_hbm, wd_hbm, wu_hbm, co_hbm,
    eg_hbm, a_hbm, b_hbm,
    ts, tt, tc, x, g, w1, w2, wd, wu, co, in_sem,
    d1, d2, h1t, xt, states, pd, proj, ag_s, ag_r, as_s, as_r,
    sl, tl, prev_s, prev_t, last_t, idx,
    comb, agg, upcot, aggcot,
    sib_snd, sib_rcv, rs_snd, rs_rcv, rb_s, rb_r, rr_s, rr_r,
    downcot, sc, second, first, gx, eg, eg_sem, out_sem,
    *ar,
):
    p = Place()
    barrier = pltpu.get_barrier_semaphore()
    partners = p.partners()
    for dev in partners:
        pl.semaphore_signal(barrier, inc=1, device_id=dev, device_id_type=MESH)
    head, tail = pl.ds(0, RB), pl.ds(RB, ROWS - RB)
    pairs = (
        (x_hbm.at[head], x.at[head]), (w1_hbm, w1), (w2_hbm, w2), (wd_hbm, wd), (x_hbm.at[tail], x.at[tail]),
        (ts_hbm, ts), (tt_hbm, tt), (tc_hbm, tc), (co_hbm, co), (wu_hbm, wu), (g_hbm, g),
    )
    loads = [pltpu.make_async_copy(s, t, in_sem.at[i]) for i, (s, t) in enumerate(pairs)]
    for c in loads:
        c.start()

    def block(zi, core, ch, n=CH):
        return proj.at[pl.ds((zi * 2 + core) * TILES + ch * CH, n)]

    def ring(side, step, ch):
        b = block(p.zat(-step if side == 0 else step), p.c, ch)
        return pltpu.make_async_remote_copy(
            src_ref=b, dst_ref=b, send_sem=ag_s.at[side, step, ch], recv_sem=ag_r.at[side, step, ch],
            device_id=p.zdev(1 if side == 0 else -1), device_id_type=MESH,
        )

    def ring_arrival(side, step, ch):
        b = block(p.zat(-1 - step if side == 0 else 1 + step), p.c, ch)
        pltpu.make_async_remote_copy(
            src_ref=b, dst_ref=b, send_sem=ag_s.at[side, step, ch], recv_sem=ag_r.at[side, step, ch],
            device_id=p.sib, device_id_type=MESH,
        ).wait_recv()

    def share(off, ch, core):
        b = block(p.zat(off), core, ch)
        k = off % NZ
        return pltpu.make_async_remote_copy(
            src_ref=b, dst_ref=b, send_sem=as_s.at[k, ch], recv_sem=as_r.at[k, ch],
            device_id=p.sib, device_id_type=MESH,
        )

    def forward(i):
        rows = pl.ds(i * RB, RB) if isinstance(i, int) else rows_at(i * RB, RB, RB)
        m = x[rows, :]
        v1 = dot(m, w1[...])
        h = (v1 * sigmoid(v1)).astype(BF16)
        d1[rows, :] = v1
        v2 = dot(h, w2[...])
        st = (m.astype(F32) + v2 * sigmoid(v2)).astype(BF16)
        d2[rows, :] = v2
        first[rows, :] = h
        states[rows, :] = st
        vd = dotg(wd[...], st, LAST)
        pr = (vd * sigmoid(vd)).astype(BF16)
        for j in range(CH):
            pd[i * CH + j] = vd[:, j * TILE:(j + 1) * TILE]
            proj[p.g * TILES + i * CH + j] = pr[:, j * TILE:(j + 1) * TILE]

    def send_own(i):
        ring(0, 0, i).start()
        ring(1, 0, i).start()
        share(0, i, p.c).start()

    for i in range(4):
        loads[i].wait()
    forward(0)
    pl.semaphore_wait(barrier, len(partners))
    send_own(0)
    loads[4].wait()

    @pl.loop(1, NCH)
    def _(i):
        forward(i)
        send_own(i)

    for i in (5, 6, 7):
        loads[i].wait()

    count = tc[0]
    for k in range(SLOTS):
        live = k < count
        sl[k] = jnp.where(live, ts[k], -1)
        tl[k] = jnp.where(live, tt[k], -1)
    for k in range(SLOTS):
        a = jnp.int32(SLOTS)
        b = jnp.int32(SLOTS)
        for e in range(k):
            a = jnp.where(sl[e] == ts[k], e, a)
            b = jnp.where(tl[e] == tt[k], e, b)
        prev_s[k] = a
        prev_t[k] = b
    for j in range(TILES):
        a = jnp.int32(SLOTS)
        for k in range(SLOTS):
            a = jnp.where(tl[k] == j, k, a)
        last_t[j] = a

    def tables(lo, hi):
        @pl.loop(lo, hi)
        def _(j):
            a = jnp.int32(SLOTS)
            for k in range(SLOTS):
                a = jnp.where(sl[k] == j, k, a)
            idx[j] = a

    def side_work(u):
        n = ROWS // (HALF * NCH)
        rows = pl.ds(u * n, n)
        d1[rows, :] = silu_grad(d1[rows, :])
        d2[rows, :] = silu_grad(d2[rows, :])
        tables(u * 2 * NZ * TILES // (HALF * NCH), (u + 1) * 2 * NZ * TILES // (HALF * NCH))
        if u % 2 == 0:
            rows = pl.ds(u * n, 2 * n)
            h1t[:, rows] = first[rows, :].T
            xt[:, rows] = x[rows, :].T

    comb[SLOTS] = jnp.zeros((TW, TILE), F32)

    for s in range(HALF):
        for ch in range(NCH):
            side_work(s * NCH + ch)
            for side in (0, 1):
                mine = (side == 0) == (ch < NCH // 2)
                if s == HALF - 1 and not mine:
                    continue
                ring_arrival(side, s, ch)
                if s + 1 < HALF - 1 or (s + 1 == HALF - 1 and mine):
                    ring(side, s + 1, ch).start()
                share(-1 - s if side == 0 else 1 + s, ch, p.c).start()

    for off in range(NZ):
        for ch in range(NCH):
            share(off, ch, 1 - p.c).wait_recv()

    loads[8].wait()
    for k in range(SLOTS):
        part = dotg(proj[ts[k]], co[k], LAST)
        comb[k] = part + comb[prev_t[k]]
    for j in range(TILES):
        agg[:, j * TILE:(j + 1) * TILE] = comb[last_t[j]].astype(BF16)

    loads[9].wait()
    loads[10].wait()

    @pl.loop(0, NCH)
    def _(i):
        rows = rows_at(i * RB, RB, RB)
        pu = dotg(agg[:, rows], wu[...], FIRST)
        uc = (g[rows, :].astype(F32) * silu_grad(pu)).astype(BF16)
        upcot[rows, :] = uc
        ac = dotg(wu[...], uc, LAST).astype(BF16)
        for j in range(CH):
            aggcot[i * CH + j] = ac[:, j * TILE:(j + 1) * TILE]

    for k in range(SLOTS):
        part = dot(aggcot[tt[k]], co[k])
        comb[k] = part + comb[prev_s[k]]

    def sib_copy(off):
        k = off % NZ
        return pltpu.make_async_remote_copy(
            src_ref=sib_snd.at[k], dst_ref=sib_rcv.at[k], send_sem=rb_s.at[k], recv_sem=rb_r.at[k],
            device_id=p.sib, device_id_type=MESH,
        )

    def red(side, step, ch):
        return pltpu.make_async_remote_copy(
            src_ref=rs_snd.at[side, step, pl.ds(ch * CH, CH)], dst_ref=rs_rcv.at[side, step, pl.ds(ch * CH, CH)],
            send_sem=rr_s.at[side, step, ch], recv_sem=rr_r.at[side, step, ch],
            device_id=p.zdev(1 if side == 0 else -1), device_id_type=MESH,
        )

    def for_sibling(off):
        base = (p.zat(off) * 2 + 1 - p.c) * TILES
        for j in range(TILES):
            sib_snd[off % NZ, j] = comb[idx[base + j]].astype(BF16)
        sib_copy(off).start()

    for_sibling(HALF)
    for s in range(HALF):
        if s + 1 < HALF:
            for_sibling(HALF - 1 - s)
            for_sibling(s + 1 - HALF)
        else:
            for_sibling(0)
        sib_copy(HALF - s).wait_recv()
        if s > 0:
            sib_copy(s - HALF).wait_recv()
        for ch in range(NCH):
            for side in (0, 1):
                off = HALF - s if side == 0 else s - HALF
                base = (p.zat(off) * 2 + p.c) * TILES
                mine = (side == 0) == (ch < NCH // 2)
                if s == 0 and not mine:
                    continue
                more = s > 1 or (s == 1 and mine)
                if more:
                    red(side, s - 1, ch).wait_recv()
                for j in range(ch * CH, ch * CH + CH):
                    v = comb[idx[base + j]] + sib_rcv[off % NZ, j].astype(F32)
                    if more:
                        v = v + rs_rcv[side, s - 1, j].astype(F32)
                    rs_snd[side, s, j] = v.astype(BF16)
                red(side, s, ch).start()
        if s == HALF - 1:
            gu = dot(agg[...], upcot[...])
            for b in range(D // TILE):
                gx[b * TILE:b * TILE + TW, :] = gu[:, b * TILE:(b + 1) * TILE]

    sib_copy(0).wait_recv()
    base = p.g * TILES
    for ch in range(NCH):
        red(0, HALF - 1, ch).wait_recv()
        red(1, HALF - 1, ch).wait_recv()
        for j in range(ch * CH, ch * CH + CH):
            v = comb[idx[base + j]] + sib_rcv[0, j].astype(F32)
            v = v + rs_rcv[0, HALF - 1, j].astype(F32) + rs_rcv[1, HALF - 1, j].astype(F32)
            downcot[:, j * TILE:(j + 1) * TILE] = (v * silu_grad(pd[j])).astype(BF16)

    @pl.loop(0, NCH)
    def _(i):
        rows = rows_at(i * RB, RB, RB)
        v = g[rows, :].astype(F32) + dotg(downcot[:, rows], wd[...], FIRST)
        sc[rows, :] = v
        second[rows, :] = (v * d2[rows, :]).astype(BF16)

    gd = dot(downcot[...], states[...])
    for b in range(D // TILE):
        gx[b * TILE + TW:(b + 1) * TILE, :] = gd[:, b * TILE:(b + 1) * TILE]

    n = len(ar) // 2
    ar_a = AllReduce(p, ar[:n - 2], ar[n - 2:n])
    ar_b = AllReduce(p, ar[n:2 * n - 2], ar[2 * n - 2:])
    h = D // 2
    theirs, own = rows_at((1 - p.c) * h, h, h), rows_at(p.c * h, h, h)
    ar_b.snd1[:, :D] = dot(h1t[theirs, :], second[...]).astype(BF16)
    ar_b.snd1[:, D:] = gx[theirs, :].astype(BF16)
    ar_b.to_sibling()
    ar_b.acc[:, :D] = dot(h1t[own, :], second[...])
    ar_b.acc[:, D:] = gx[own, :]

    @pl.loop(0, NCH)
    def _(i):
        rows = rows_at(i * RB, RB, RB)
        v = dotg(second[rows, :], w2[...], LAST)
        first[rows, :] = (v * d1[rows, :]).astype(BF16)

    ar_b.to_plane()
    ar_a.snd1[...] = dot(xt[theirs, :], first[...]).astype(BF16)
    ar_a.to_sibling()
    ar_a.acc[...] = dot(xt[own, :], first[...])

    def eg_copy(i):
        rows = rows_at(i * RB, RB, RB)
        return pltpu.make_async_copy(eg.at[rows, :], eg_hbm.at[rows, :], eg_sem.at[i])

    def edges(lo, hi):
        @pl.loop(lo, hi)
        def _(i):
            rows = rows_at(i * RB, RB, RB)
            v = sc[rows, :] + dotg(first[rows, :], w1[...], LAST)
            eg[rows, :] = v.astype(BF16)
            eg_copy(i).start()

    edges(0, 1)
    ar_a.to_plane()
    edges(1, 2)
    ar_b.to_column()
    edges(2, NCH)
    ar_a.to_column()
    ar_b.plane_back()
    ar_a.plane_back()
    ar_b.sibling_back()
    ar_a.sibling_back()
    ar_b.end()
    ob = pltpu.make_async_copy(ar_b.fin, b_hbm, out_sem.at[1])
    ob.start()
    ar_a.end()
    oa = pltpu.make_async_copy(ar_a.fin, a_hbm, out_sem.at[0])
    oa.start()

    for ch in range(NCH):
        for side in (0, 1):
            for s in range(HALF):
                mine = (side == 0) == (ch < NCH // 2)
                if s < HALF - 1 or mine:
                    ring(side, s, ch).wait_send()
                if s > 0 or mine:
                    red(side, s, ch).wait_send()
        for off in range(NZ):
            share(off, ch, p.c).wait_send()
        eg_copy(ch).wait()
    for off in range(NZ):
        sib_copy(off).wait_send()
    ar_a.close()
    ar_b.close()
    ob.wait()
    oa.wait()


def ar_scratch(w):
    h = D // 2
    return [
        pltpu.VMEM((h, w), BF16), pltpu.VMEM((h, w), BF16), pltpu.VMEM((h, w), F32), pltpu.VMEM((h, w), BF16),
        pltpu.VMEM((N_DP, PIECE, w), BF16), pltpu.VMEM((NZ, PIECE, w), BF16), pltpu.VMEM((D, w), BF16),
        pltpu.SemaphoreType.DMA((42,)), pltpu.SemaphoreType.DMA((42,)),
    ]


def widen(e_in, a_in, b_in, e_out, a_out, b_out, d_out, u_out, e, a, b, fa, fb, fd, fu, in_sem, out_sem, e_sem):
    n = 4
    parts = [pl.ds(i * (ROWS // n), ROWS // n) for i in range(n)]
    la = pltpu.make_async_copy(a_in, a, in_sem.at[0])
    lb = pltpu.make_async_copy(b_in, b, in_sem.at[1])
    le = [pltpu.make_async_copy(e_in.at[r], e.at[r], in_sem.at[2 + i]) for i, r in enumerate(parts)]
    se = [pltpu.make_async_copy(e.at[r], e_out.at[r], e_sem.at[i]) for i, r in enumerate(parts)]
    outs = [
        pltpu.make_async_copy(s, t, out_sem.at[i])
        for i, (s, t) in enumerate(((fa, a_out), (fb, b_out), (fd, d_out), (fu, u_out)))
    ]
    for c in [la, lb] + le:
        c.start()
    la.wait()
    fa[...] = a[...].astype(F32)
    outs[0].start()
    lb.wait()
    fb[...] = b[:, :D].astype(F32)
    outs[1].start()
    for k in range(D // TILE):
        cols = pl.ds(k * TILE, TILE)
        fu[:, cols] = b[k * TILE:k * TILE + TW, D:].astype(F32)
        fd[:, cols] = b[k * TILE + TW:(k + 1) * TILE, D:].astype(F32)
    outs[2].start()
    outs[3].start()
    for i in range(n):
        le[i].wait()
        se[i].start()
    for c in se + outs:
        c.wait()


def on_device(
    edge_in, cotangent, weight_first, weight_second, weight_down, weight_up,
    coeffs, tile_source, tile_target, tile_count,
):
    V, S = pltpu.VMEM, pltpu.SMEM
    dma = pltpu.SemaphoreType.DMA
    scratch = [
        S((SLOTS,), jnp.int32), S((SLOTS,), jnp.int32), S((1,), jnp.int32),
        V((ROWS, D), BF16), V((ROWS, D), BF16), V((D, D), BF16), V((D, D), BF16),
        V((TW, D), BF16), V((TW, D), BF16), V((SLOTS, TILE, TILE), BF16), dma((11,)),
        V((ROWS, D), F32), V((ROWS, D), F32), V((D, ROWS), BF16), V((D, ROWS), BF16),
        V((ROWS, D), BF16), V((TILES, TW, TILE), F32), V((2 * NZ * TILES, TW, TILE), BF16),
        dma((2, HALF, NCH)), dma((2, HALF, NCH)), dma((NZ, NCH)), dma((NZ, NCH)),
        S((SLOTS,), jnp.int32), S((SLOTS,), jnp.int32), S((SLOTS,), jnp.int32), S((SLOTS,), jnp.int32),
        S((TILES,), jnp.int32), S((2 * NZ * TILES,), jnp.int32),
        V((SLOTS + 1, TW, TILE), F32), V((TW, ROWS), BF16), V((ROWS, D), BF16), V((TILES, TW, TILE), BF16),
        V((NZ, TILES, TW, TILE), BF16), V((NZ, TILES, TW, TILE), BF16),
        V((2, HALF, TILES, TW, TILE), BF16), V((2, HALF, TILES, TW, TILE), BF16),
        dma((NZ,)), dma((NZ,)), dma((2, HALF, NCH)), dma((2, HALF, NCH)),
        V((TW, ROWS), BF16), V((ROWS, D), F32), V((ROWS, D), BF16), V((ROWS, D), BF16),
        V((D, EXTRA), F32), V((ROWS, D), BF16), dma((NCH,)), dma((2,)),
    ] + ar_scratch(D) + ar_scratch(WB)
    hbm = pl.BlockSpec(memory_space=pl.ANY)
    edge_grad, a, b = pl.pallas_call(
        kernel,
        out_shape=(
            jax.ShapeDtypeStruct((ROWS, D), BF16),
            jax.ShapeDtypeStruct((D, D), BF16),
            jax.ShapeDtypeStruct((D, WB), BF16),
        ),
        in_specs=[hbm] * 10,
        out_specs=(hbm,) * 3,
        scratch_shapes=scratch,
        compiler_params=pltpu.CompilerParams(
            collective_id=0, has_side_effects=True, vmem_limit_bytes=56 * 1024 * 1024
        ),
        cost_estimate=pl.CostEstimate(flops=7_400_000_000, bytes_accessed=8_000_000, transcendentals=2_000_000),
    )(
        tile_source, tile_target, tile_count, edge_in, cotangent, weight_first, weight_second,
        weight_down, weight_up, coeffs,
    )
    grad = jax.ShapeDtypeStruct((D, D), F32)
    small = jax.ShapeDtypeStruct((TW, D), F32)
    return pl.pallas_call(
        widen,
        out_shape=(jax.ShapeDtypeStruct((ROWS, D), BF16), grad, grad, small, small),
        in_specs=[hbm] * 3,
        out_specs=(hbm,) * 5,
        scratch_shapes=[
            V((ROWS, D), BF16), V((D, D), BF16), V((D, WB), BF16),
            V((D, D), F32), V((D, D), F32), V((TW, D), F32), V((TW, D), F32),
            dma((6,)), dma((4,)), dma((4,)),
        ],
        compiler_params=pltpu.CompilerParams(vmem_limit_bytes=60 * 1024 * 1024),
        cost_estimate=pl.CostEstimate(flops=600_000, bytes_accessed=5_700_000, transcendentals=0),
    )(edge_grad, a, b)


def solution(mesh):
    return jax.shard_map(
        on_device,
        mesh=mesh,
        in_specs=(
            P(("dp", "graph"), None), P(("dp", "graph"), None), P(), P(), P(), P(),
            P(("dp", "graph"), None, None), P(("dp", "graph")), P(("dp", "graph")), P(("dp", "graph")),
        ),
        out_specs=(P(("dp", "graph"), None), P(), P(), P(), P()),
        check_vma=False,
    )
```

time: 95.7 us -> 83.3 us (0.87)
  Pallas kernels: 88.5 us -> 81.9 us
  local copies, waits for them, and re-layouts: 3.48 us -> 0 us
  other arithmetic: 2.22 us -> 0 us
    pallas_call x1, Pallas kernels: 88.5 us -> 78.9 us  [on_device(): pl.pallas_call(kernel, out_shape=(jax.ShapeDtypeStruct((ROWS, D), BF16),...]
    pallas_call x0 -> x1, Pallas kernels: none -> 2.98 us  [on_device(): pl.pallas_call(widen, out_shape=(jax.ShapeDtypeStruct((ROWS, D), BF16), g...]
    convert_element_type x3 -> x0, other arithmetic: 2.22 us -> none  [the longest x2 2.2 us: on_device(): return (edge_grad, a.astype(F32), b[:, :D].astype(F32), extra[1], extra[0])]
    unnamed x7 -> x0, local copies, waits for them, and re-layouts: 1.65 us -> none
    slice x4 -> x0, local copies, waits for them, and re-layouts: 1.11 us -> none  [the longest x1 0.91 us: on_device(): b[:, D:].reshape(D // TILE, 2, TW, TILE).transpose(1, 2, 0, 3)]
where the time goes in v2:
time: 83.3 us; the launch traced here: 83.2 us
  Pallas kernels  81.9 us (98%)
  between operations  1.29 us (2%)
    pallas_call x1, Pallas kernels, on_device(): pl.pallas_call(kernel, out_shape=(jax.ShapeDtypeStruct((ROWS, D), BF16),...  78.9 us
    pallas_call x1, Pallas kernels, on_device(): pl.pallas_call(widen, out_shape=(jax.ShapeDtypeStruct((ROWS, D), BF16), g...  2.98 us

profile of v2, /device:TPU:1, one launch (start us, length us, event | category | flops | bytes accessed | tf_op | source)
XLA Modules:
  0.0 83.2 jit_solution(3601117099187606046)
XLA Ops:
  1.3 78.9 %shard_map.137 = (bf16[1024,512]{1,0:T(8,128)(2,1)}, bf16[512,512]{1,0:T(8,128)(2,1)}, bf16[512,640]{1,0:T(8,128)(2,1)}) custom-call(s32[24]{0:T(128)} %ts_hbm.1, s32[24]{0:T(128)} %tt_hbm.1, s32[1]{0:T(128)S(6)} %copy.15.tc_hbm, bf16[1024,512]{1,0:T(8,128)(2,1)} %x_hbm.1, bf16[1024,512]{1,0:T(8,128)(2,1)} %g_hbm.1, bf16[512,512]{1,0:T(8,128)(2,1)} %w1_hbm.1, ...), custom_call_target="tpu_custom_call" | custom-call | flops 7400000000 | bytes 8000000 | tf_op jit(solution)/shard_map/pallas_call | solution.py:530
  80.2 3.0 %shard_map.138 = (bf16[1024,512]{1,0:T(8,128)(2,1)}, f32[512,512]{1,0:T(8,128)}, f32[512,512]{1,0:T(8,128)}, f32[64,512]{1,0:T(8,128)}, f32[64,512]{1,0:T(8,128)}) custom-call(bf16[1024,512]{1,0:T(8,128)(2,1)} %get-tuple-element.8.e_in, bf16[512,512]{1,0:T(8,128)(2,1)} %get-tuple-element.9.a_in, bf16[512,640]{1,0:T(8,128)(2,1)} %get-tuple-element.10.b_in), custom_call_target="tpu_custom_call" | custom-call | flops 600000 | bytes 5700000 | tf_op jit(solution)/shard_map/pallas_call | solution.py:550

commit v3 on v2

--- a/solution.py
+++ b/solution.py
@@ -123,9 +123,11 @@
             ys = lax.rem(p.y + NY - dy, NY)
             self.arrived(self.part(1 - p.c, ys * NX, NX), 38 + dy)
 
-    def close(self):
-        for c in self.open:
+    def close(self, keep=0):
+        n = len(self.open) - keep
+        for c in self.open[:n]:
             c.wait_send()
+        self.open = self.open[n:]
 
 
 class Place:
@@ -159,7 +161,7 @@
     eg_hbm, a_hbm, b_hbm,
     ts, tt, tc, x, g, w1, w2, wd, wu, co, in_sem,
     d1, d2, h1t, xt, states, pd, proj, ag_s, ag_r, as_s, as_r,
-    sl, tl, prev_s, prev_t, last_t, idx,
+    tab_v, tab,
     comb, agg, upcot, aggcot,
     sib_snd, sib_rcv, rs_snd, rs_rcv, rb_s, rb_r, rr_s, rr_r,
     downcot, sc, second, first, gx, eg, eg_sem, out_sem,
@@ -183,10 +185,11 @@
         return proj.at[pl.ds((zi * 2 + core) * TILES + ch * CH, n)]
 
     def ring(side, step, ch):
-        b = block(p.zat(-step if side == 0 else step), p.c, ch)
+        back, on = (step, 1) if step < HALF - 1 else (HALF - 2, 2)
+        b = block(p.zat(-back if side == 0 else back), p.c, ch)
         return pltpu.make_async_remote_copy(
             src_ref=b, dst_ref=b, send_sem=ag_s.at[side, step, ch], recv_sem=ag_r.at[side, step, ch],
-            device_id=p.zdev(1 if side == 0 else -1), device_id_type=MESH,
+            device_id=p.zdev(on if side == 0 else -on), device_id_type=MESH,
         )
 
     def ring_arrival(side, step, ch):
@@ -242,40 +245,34 @@
         loads[i].wait()
 
     count = tc[0]
+    lane = lax.broadcasted_iota(jnp.int32, (1, TILE), 1)
+    none = jnp.full((1, TILE), SLOTS, jnp.int32)
+    sv = tv = jnp.zeros((1, TILE), jnp.int32)
+    for k in range(SLOTS):
+        sv = jnp.where(lane == k, ts[k], sv)
+        tv = jnp.where(lane == k, tt[k], tv)
+    before_s = before_t = final_s = final_t = none
     for k in range(SLOTS):
         live = k < count
-        sl[k] = jnp.where(live, ts[k], -1)
-        tl[k] = jnp.where(live, tt[k], -1)
-    for k in range(SLOTS):
-        a = jnp.int32(SLOTS)
-        b = jnp.int32(SLOTS)
-        for e in range(k):
-            a = jnp.where(sl[e] == ts[k], e, a)
-            b = jnp.where(tl[e] == tt[k], e, b)
-        prev_s[k] = a
-        prev_t[k] = b
-    for j in range(TILES):
-        a = jnp.int32(SLOTS)
-        for k in range(SLOTS):
-            a = jnp.where(tl[k] == j, k, a)
-        last_t[j] = a
-
-    def tables(lo, hi):
-        @pl.loop(lo, hi)
-        def _(j):
-            a = jnp.int32(SLOTS)
-            for k in range(SLOTS):
-                a = jnp.where(sl[k] == j, k, a)
-            idx[j] = a
+        sk = jnp.where(live, ts[k], -1)
+        tk = jnp.where(live, tt[k], -1)
+        later = lane > k
+        before_s = jnp.where(later & (sv == sk), k, before_s)
+        before_t = jnp.where(later & (tv == tk), k, before_t)
+        final_s = jnp.where(lane == sk, k, final_s)
+        final_t = jnp.where(lane == tk, k, final_t)
+    for i, v in enumerate((final_s, before_s, before_t, final_t, none, none, none, none)):
+        tab_v[i:i + 1, :] = v
+    to_scalar = pltpu.make_async_copy(tab_v, tab, in_sem.at[11])
+    to_scalar.start()
 
     def side_work(u):
         n = ROWS // (HALF * NCH)
         rows = pl.ds(u * n, n)
         d1[rows, :] = silu_grad(d1[rows, :])
         d2[rows, :] = silu_grad(d2[rows, :])
-        tables(u * 2 * NZ * TILES // (HALF * NCH), (u + 1) * 2 * NZ * TILES // (HALF * NCH))
-        if u % 2 == 0:
-            rows = pl.ds(u * n, 2 * n)
+        if u * n % TILE == 0:
+            rows = pl.ds(u * n, TILE)
             h1t[:, rows] = first[rows, :].T
             xt[:, rows] = x[rows, :].T
 
@@ -289,7 +286,9 @@
                 if s == HALF - 1 and not mine:
                     continue
                 ring_arrival(side, s, ch)
-                if s + 1 < HALF - 1 or (s + 1 == HALF - 1 and mine):
+                if s == HALF - 3 and mine:
+                    ring(side, HALF - 1, ch).start()
+                if s < HALF - 2:
                     ring(side, s + 1, ch).start()
                 share(-1 - s if side == 0 else 1 + s, ch, p.c).start()
 
@@ -298,11 +297,12 @@
             share(off, ch, 1 - p.c).wait_recv()
 
     loads[8].wait()
+    to_scalar.wait()
     for k in range(SLOTS):
         part = dotg(proj[ts[k]], co[k], LAST)
-        comb[k] = part + comb[prev_t[k]]
+        comb[k] = part + comb[tab[2, k]]
     for j in range(TILES):
-        agg[:, j * TILE:(j + 1) * TILE] = comb[last_t[j]].astype(BF16)
+        agg[:, j * TILE:(j + 1) * TILE] = comb[tab[3, j]].astype(BF16)
 
     loads[9].wait()
     loads[10].wait()
@@ -319,7 +319,7 @@
 
     for k in range(SLOTS):
         part = dot(aggcot[tt[k]], co[k])
-        comb[k] = part + comb[prev_s[k]]
+        comb[k] = part + comb[tab[1, k]]
 
     def sib_copy(off):
         k = off % NZ
@@ -329,16 +329,17 @@
         )
 
     def red(side, step, ch):
+        on = 1 if step else 2
         return pltpu.make_async_remote_copy(
             src_ref=rs_snd.at[side, step, pl.ds(ch * CH, CH)], dst_ref=rs_rcv.at[side, step, pl.ds(ch * CH, CH)],
             send_sem=rr_s.at[side, step, ch], recv_sem=rr_r.at[side, step, ch],
-            device_id=p.zdev(1 if side == 0 else -1), device_id_type=MESH,
+            device_id=p.zdev(on if side == 0 else -on), device_id_type=MESH,
         )
 
     def for_sibling(off):
         base = (p.zat(off) * 2 + 1 - p.c) * TILES
         for j in range(TILES):
-            sib_snd[off % NZ, j] = comb[idx[base + j]].astype(BF16)
+            sib_snd[off % NZ, j] = comb[tab[0, base + j]].astype(BF16)
         sib_copy(off).start()
 
     for_sibling(HALF)
@@ -351,20 +352,23 @@
         sib_copy(HALF - s).wait_recv()
         if s > 0:
             sib_copy(s - HALF).wait_recv()
-        for ch in range(NCH):
+        for q in range(NCH):
             for side in (0, 1):
+                ch = (q + NCH // 2) % NCH if side == 0 else q
                 off = HALF - s if side == 0 else s - HALF
                 base = (p.zat(off) * 2 + p.c) * TILES
                 mine = (side == 0) == (ch < NCH // 2)
                 if s == 0 and not mine:
                     continue
-                more = s > 1 or (s == 1 and mine)
-                if more:
-                    red(side, s - 1, ch).wait_recv()
+                joins = [s - 1] if s > 1 else []
+                if s == 2 and mine:
+                    joins.append(0)
+                for e in joins:
+                    red(side, e, ch).wait_recv()
                 for j in range(ch * CH, ch * CH + CH):
-                    v = comb[idx[base + j]] + sib_rcv[off % NZ, j].astype(F32)
-                    if more:
-                        v = v + rs_rcv[side, s - 1, j].astype(F32)
+                    v = comb[tab[0, base + j]] + sib_rcv[off % NZ, j].astype(F32)
+                    for e in joins:
+                        v = v + rs_rcv[side, e, j].astype(F32)
                     rs_snd[side, s, j] = v.astype(BF16)
                 red(side, s, ch).start()
         if s == HALF - 1:
@@ -378,7 +382,7 @@
         red(0, HALF - 1, ch).wait_recv()
         red(1, HALF - 1, ch).wait_recv()
         for j in range(ch * CH, ch * CH + CH):
-            v = comb[idx[base + j]] + sib_rcv[0, j].astype(F32)
+            v = comb[tab[0, base + j]] + sib_rcv[0, j].astype(F32)
             v = v + rs_rcv[0, HALF - 1, j].astype(F32) + rs_rcv[1, HALF - 1, j].astype(F32)
             downcot[:, j * TILE:(j + 1) * TILE] = (v * silu_grad(pd[j])).astype(BF16)
 
@@ -427,22 +431,10 @@
             eg[rows, :] = v.astype(BF16)
             eg_copy(i).start()
 
-    edges(0, 1)
+    edges(0, 2)
+    ar_b.to_column()
     ar_a.to_plane()
-    edges(1, 2)
-    ar_b.to_column()
     edges(2, NCH)
-    ar_a.to_column()
-    ar_b.plane_back()
-    ar_a.plane_back()
-    ar_b.sibling_back()
-    ar_a.sibling_back()
-    ar_b.end()
-    ob = pltpu.make_async_copy(ar_b.fin, b_hbm, out_sem.at[1])
-    ob.start()
-    ar_a.end()
-    oa = pltpu.make_async_copy(ar_a.fin, a_hbm, out_sem.at[0])
-    oa.start()
 
     for ch in range(NCH):
         for side in (0, 1):
@@ -454,11 +446,29 @@
                     red(side, s, ch).wait_send()
         for off in range(NZ):
             share(off, ch, p.c).wait_send()
-        eg_copy(ch).wait()
     for off in range(NZ):
         sib_copy(off).wait_send()
+
+    ar_b.plane_back()
+    ar_a.to_column()
+    ar_b.close(N_DP - 1)
+    ar_a.close(NZ - 1)
+    ar_a.plane_back()
+    ar_b.close()
+    ar_a.close(N_DP - 1)
+    ar_b.sibling_back()
+    ar_a.sibling_back()
+    ar_b.end()
+    ob = pltpu.make_async_copy(ar_b.fin, b_hbm, out_sem.at[1])
+    ob.start()
+    ar_a.end()
+    oa = pltpu.make_async_copy(ar_a.fin, a_hbm, out_sem.at[0])
+    oa.start()
+
+    for i in range(NCH):
+        eg_copy(i).wait()
+    ar_b.close()
     ar_a.close()
-    ar_b.close()
     ob.wait()
     oa.wait()
 
@@ -513,12 +523,11 @@
     scratch = [
         S((SLOTS,), jnp.int32), S((SLOTS,), jnp.int32), S((1,), jnp.int32),
         V((ROWS, D), BF16), V((ROWS, D), BF16), V((D, D), BF16), V((D, D), BF16),
-        V((TW, D), BF16), V((TW, D), BF16), V((SLOTS, TILE, TILE), BF16), dma((11,)),
+        V((TW, D), BF16), V((TW, D), BF16), V((SLOTS, TILE, TILE), BF16), dma((12,)),
         V((ROWS, D), F32), V((ROWS, D), F32), V((D, ROWS), BF16), V((D, ROWS), BF16),
         V((ROWS, D), BF16), V((TILES, TW, TILE), F32), V((2 * NZ * TILES, TW, TILE), BF16),
         dma((2, HALF, NCH)), dma((2, HALF, NCH)), dma((NZ, NCH)), dma((NZ, NCH)),
-        S((SLOTS,), jnp.int32), S((SLOTS,), jnp.int32), S((SLOTS,), jnp.int32), S((SLOTS,), jnp.int32),
-        S((TILES,), jnp.int32), S((2 * NZ * TILES,), jnp.int32),
+        V((8, TILE), jnp.int32), S((8, TILE), jnp.int32),
         V((SLOTS + 1, TW, TILE), F32), V((TW, ROWS), BF16), V((ROWS, D), BF16), V((TILES, TW, TILE), BF16),
         V((NZ, TILES, TW, TILE), BF16), V((NZ, TILES, TW, TILE), BF16),
         V((2, HALF, TILES, TW, TILE), BF16), V((2, HALF, TILES, TW, TILE), BF16),

time: 83.3 us -> 81.8 us (0.982)
  Pallas kernels: 81.9 us -> 80.6 us
    pallas_call x1, Pallas kernels: 78.9 us -> 77.6 us  [on_device(): pl.pallas_call(kernel, out_shape=(jax.ShapeDtypeStruct((ROWS, D), BF16),...]
where the time goes in v3:
time: 81.8 us; the launch traced here: 81.9 us
  Pallas kernels  80.6 us (99%)
  between operations  1.29 us (2%)
    pallas_call x1, Pallas kernels, on_device(): pl.pallas_call(kernel, out_shape=(jax.ShapeDtypeStruct((ROWS, D), BF16),...  77.6 us
    pallas_call x1, Pallas kernels, on_device(): pl.pallas_call(widen, out_shape=(jax.ShapeDtypeStruct((ROWS, D), BF16), g...  2.98 us

profile of v3, /device:TPU:1, one launch (start us, length us, event | category | flops | bytes accessed | tf_op | source)
XLA Modules:
  0.0 81.9 jit_solution(10077550956103422770)
XLA Ops:
  1.3 77.6 %shard_map.137 = (bf16[1024,512]{1,0:T(8,128)(2,1)}, bf16[512,512]{1,0:T(8,128)(2,1)}, bf16[512,640]{1,0:T(8,128)(2,1)}) custom-call(s32[24]{0:T(128)} %ts_hbm.1, s32[24]{0:T(128)} %tt_hbm.1, s32[1]{0:T(128)S(6)} %copy.15.tc_hbm, bf16[1024,512]{1,0:T(8,128)(2,1)} %x_hbm.1, bf16[1024,512]{1,0:T(8,128)(2,1)} %g_hbm.1, bf16[512,512]{1,0:T(8,128)(2,1)} %w1_hbm.1, ...), custom_call_target="tpu_custom_call" | custom-call | flops 7400000000 | bytes 8000000 | tf_op jit(solution)/shard_map/pallas_call | solution.py:539
  78.9 3.0 %shard_map.138 = (bf16[1024,512]{1,0:T(8,128)(2,1)}, f32[512,512]{1,0:T(8,128)}, f32[512,512]{1,0:T(8,128)}, f32[64,512]{1,0:T(8,128)}, f32[64,512]{1,0:T(8,128)}) custom-call(bf16[1024,512]{1,0:T(8,128)(2,1)} %get-tuple-element.8.e_in, bf16[512,512]{1,0:T(8,128)(2,1)} %get-tuple-element.9.a_in, bf16[512,640]{1,0:T(8,128)(2,1)} %get-tuple-element.10.b_in), custom_call_target="tpu_custom_call" | custom-call | flops 600000 | bytes 5700000 | tf_op jit(solution)/shard_map/pallas_call | solution.py:559
